TPU v7x, 512 devices: a whole 4x4x16 slice. The times are simulated.
512 devices in a mesh: gx: 16 (over z), gy: 32 (over y, x, core).
Axes of the slice: x: 4, y: 4, z: 16, core: 2. Of those that a mesh axis runs over, the one named last changes fastest.
Arguments:
- permeability: float32 [32, 512, 2048], P(None, 'gy', 'gx'), may hold values from 0.25 to 4
- source: float32 [32, 512, 2048], P(None, 'gy', 'gx'), may hold values from -16 to 16
- phase_mask: int32 [32, 512, 2048], P(None, 'gy', 'gx'), may hold values from 0 to 2
Outputs:
- pressure: float32 [32, 512, 2048], P(None, 'gy', 'gx')
- correction_mid: float32 [16, 256, 1024], P(None, 'gy', 'gx')
- correction_low: float32 [8, 128, 512], P(None, 'gy', 'gx')
Inputs may be any that keep to these rules, and one draw needn't show every extreme that they name: `phase_mask`: 0 liquid, 1 mushy, 2 solid.
All inputs are finite; a program needn't handle non-finite values.
Results may differ from a plain program's by a relative error of at most 0.0003.
Values sent between devices are 32-bit elements; how exact they have to be, the bound alone decides.
A program may use at most 128 MiB of HBM per device.

v0:
```python
import jax
import jax.numpy as jnp
from jax import lax
from jax.sharding import PartitionSpec as P

NU = 8
COARSE_SWEEPS = 8


RELAXATION = 0.8
STORAGE = 0.05
LEAK_SHARE = 0.1


def padded(shard, sides, width):
    for axis, dim in sides:
        size, length = (lax.axis_size(axis), shard.shape[dim])
        up = [(i, (i + 1) % size) for i in range(size - 1)]
        down = [(j, i) for i, j in up]
        last = lax.slice_in_dim(shard, length - width, length, axis=dim)
        leading = lax.slice_in_dim(shard, 0, width, axis=dim)
        before = lax.ppermute(last, axis, up)
        after = lax.ppermute(leading, axis, down)
        shard = jnp.concatenate([before, shard, after], axis=dim)
    return shard


def harmonic(lower_cell, upper_cell):
    face_sum = lower_cell + upper_cell
    divisor = jnp.where(face_sum > 0.0, face_sum, 1.0)
    return 2.0 * lower_cell * upper_cell / divisor


def extend(block, width_cells):
    return padded(block, (("gx", 3), ("gy", 2)), width_cells)


def coefficients(cond_ext, face_scale, store_scale):
    z_padded = jnp.pad(cond_ext, ((1, 1), (0, 0), (0, 0)))
    east_west = harmonic(cond_ext[:, :, :-1], cond_ext[:, :, 1:]) * face_scale
    north_south = harmonic(cond_ext[:, :-1, :], cond_ext[:, 1:, :]) * face_scale
    vertical = harmonic(z_padded[:-1], z_padded[1:]) * face_scale
    centre_cells = cond_ext[:, 1:-1, 1:-1]
    diagonal = (
        east_west[:, 1:-1, 1:]
        + east_west[:, 1:-1, :-1]
        + north_south[:, 1:, 1:-1]
        + north_south[:, :-1, 1:-1]
        + vertical[1:, 1:-1, 1:-1]
        + vertical[:-1, 1:-1, 1:-1]
        + store_scale * centre_cells
        + jnp.where(centre_cells > 0.0, 0.0, 1.0)
    )
    return (east_west, north_south, vertical, diagonal)


def operate(iterate, stencil):
    east_west, north_south, vertical, diagonal = stencil
    z_padded = jnp.pad(iterate, ((1, 1), (0, 0), (0, 0)))
    return (
        diagonal * iterate[:, 1:-1, 1:-1]
        - east_west[:, 1:-1, 1:] * iterate[:, 1:-1, 2:]
        - east_west[:, 1:-1, :-1] * iterate[:, 1:-1, :-2]
        - north_south[:, 1:, 1:-1] * iterate[:, 2:, 1:-1]
        - north_south[:, :-1, 1:-1] * iterate[:, :-2, 1:-1]
        - vertical[1:, 1:-1, 1:-1] * z_padded[2:, 1:-1, 1:-1]
        - vertical[:-1, 1:-1, 1:-1] * z_padded[:-2, 1:-1, 1:-1]
    )


def restrict(cells):
    depth_cells, row_cells, column_cells = cells.shape
    return cells.reshape(depth_cells // 2, 2, row_cells // 2, 2, column_cells // 2, 2).sum(
        axis=(1, 3, 5)
    )


def spread_level(right_side, conductance, face_scale, store_scale, sweeps):
    stencil = coefficients(extend(conductance[None], 1)[0], face_scale, store_scale)
    weight = RELAXATION / stencil[3]
    iterate = weight * right_side
    for sweep_no in range(sweeps - 1):
        iterate = iterate + weight * (right_side - operate(extend(iterate[None], 1)[0], stencil))
    return (iterate, stencil)


def per_device(permeability, source, phase_mask):
    conductance = jnp.where(phase_mask == 2, 0.0, permeability)
    right_side = jnp.where(phase_mask == 1, source, 0.0)
    stencil = coefficients(extend(conductance[None], 1)[0], 1.0, STORAGE)
    weight = RELAXATION / stencil[3]
    pressure = weight * right_side
    for sweep_no in range(NU - 1):
        pressure = pressure + weight * (right_side - operate(extend(pressure[None], 1)[0], stencil))
    residual = right_side - operate(extend(pressure[None], 1)[0], stencil)
    side_mid = restrict(residual)
    cond_mid = restrict(LEAK_SHARE * permeability + (1.0 - LEAK_SHARE) * conductance) * 0.125
    correction_mid, stencil_mid = spread_level(side_mid, cond_mid, 2.0, 8.0 * STORAGE, NU)
    side_low = restrict(side_mid - operate(extend(correction_mid[None], 1)[0], stencil_mid))
    cond_low = restrict(cond_mid) * 0.125
    correction_low, stencil_low = spread_level(
        side_low, cond_low, 4.0, 64.0 * STORAGE, COARSE_SWEEPS
    )
    return (pressure, correction_mid, correction_low)


def solution(mesh):
    placed = (P(None, "gy", "gx"), P(None, "gy", "gx"), P(None, "gy", "gx"))
    return jax.shard_map(
        per_device,
        mesh=mesh,
        in_specs=placed,
        out_specs=(P(None, "gy", "gx"), P(None, "gy", "gx"), P(None, "gy", "gx")),
        check_vma=False,
    )
```

profile of v0, /device:TPU:7, one launch (start us, length us, event | category | flops | bytes accessed | tf_op | source)
XLA Modules:
  0.0 575.3 jit_solution(520620118130882790)
XLA Ops:
  22.1 5.4 collective-permute-done.3
  37.3 5.2 collective-permute-done.5
  49.0 5.4 collective-permute-done.7
  73.5 5.4 collective-permute-done.11
  96.9 5.4 collective-permute-done.15
  120.9 5.4 collective-permute-done.19
  128.4 5.4 collective-permute-start.20
  135.3 18.8 %reshape.37 = f32[16,2,8,2,64,2]{5,4,3,2,1,0:T(8,128)} reshape(f32[32,16,128]{2,1,0:T(8,128)} %get-tuple-element.28) | data formatting | bytes 524288 | tf_op jit(solution)/shard_map/reshape | solution.py:73
  154.1 7.0 %reduce_sum.36 = f32[16,8,64]{2,1,0:T(8,128)S(1)} reduce(f32[16,2,8,2,64,2]{5,4,3,2,1,0:T(8,128)} %reshape.37, f32[]{:T(128)} %constant.15.clone.1), dimensions={1,3,5}, to_apply=%region_0.1 | reduce | flops 57344 | bytes 294916 | tf_op jit(solution)/shard_map/reduce_sum | solution.py:73
  166.9 5.2 collective-permute-done.23
  192.3 5.8 collective-permute-start.34
  212.4 6.9 %collective-permute-start.30 = (f32[1,32,1,130]{3,2,1,0:T(1,128)S(1)}, f32[1,32,1,130]{3,2,1,0:T(1,128)S(1)}, u32[]{:S(2)}, u32[]{:S(2)}) collective-permute-start(f32[1,32,1,130]{3,2,1,0:T(1,128)S(1)} %get-tuple-element.12), channel_id=1, source_target_pairs={{0,1},{1,2},{2,3},{3,4},{4,5},{5,6},{6,7},{7,8},{8,9},{9,10},{10,1... | collective-permute-start | bytes 49928 | tf_op jit(solution)/shard_map/ppermute | solution.py:22
  221.3 5.3 collective-permute-done.31
  245.2 5.1 collective-permute-done.39
  252.3 18.8 %reshape.38 = f32[16,2,8,2,64,2]{5,4,3,2,1,0:T(8,128)} reshape(f32[32,16,128]{2,1,0:T(8,128)} %fusion.55) | data formatting | bytes 524288 | tf_op jit(solution)/shard_map/reshape | solution.py:73
  271.1 7.0 %reduce_sum.37 = f32[16,8,64]{2,1,0:T(8,128)S(1)} reduce(f32[16,2,8,2,64,2]{5,4,3,2,1,0:T(8,128)} %reshape.38, f32[]{:T(128)} %constant.15.clone.1), dimensions={1,3,5}, to_apply=%region_1.2 | reduce | flops 57344 | bytes 294916 | tf_op jit(solution)/shard_map/reduce_sum | solution.py:73
  293.7 5.1 collective-permute-done.43
  313.4 5.1 collective-permute-done.47
  332.4 5.1 collective-permute-done.51
  351.4 5.1 collective-permute-done.55
  370.3 5.1 collective-permute-done.59
  390.9 5.8 collective-permute-start.70
  408.5 7.2 %collective-permute-start.66 = (f32[1,16,1,66]{3,2,1,0:T(1,128)S(1)}, f32[1,16,1,66]{3,2,1,0:T(1,128)S(1)}, u32[]{:S(2)}, u32[]{:S(2)}) collective-permute-start(f32[1,16,1,66]{3,2,1,0:T(1,128)S(1)} %get-tuple-element.50), channel_id=1, source_target_pairs={{0,1},{1,2},{2,3},{3,4},{4,5},{5,6},{6,7},{7,8},{8,9},{9,10},{10,1... | collective-permute-start | bytes 12680 | tf_op jit(solution)/shard_map/ppermute | solution.py:22
  417.6 5.1 collective-permute-done.67
  (312 shorter events, 411.6 us)
Async XLA Ops:
  2.6 8.5 %collective-permute-start = (f32[1,32,16,1]{3,2,1,0:T(8,128)S(1)}, f32[1,32,16,1]{3,2,1,0:T(8,128)S(1)}, u32[]{:S(2)}, u32[]{:S(2)}) collective-permute-start(f32[1,32,16,1]{3,2,1,0:T(8,128)S(1)} %get-tuple-element.46), channel_id=1, source_target_pairs={{0,32},{32,64},{64,96},{96,128},{128,160},{160,192},{192,224},{224... | collective-permute-start | bytes 6152 | tf_op jit(solution)/shard_map/ppermute | solution.py:22
  6.1 9.1 %collective-permute-start.1 = (f32[1,32,16,1]{3,2,1,0:T(8,128)S(1)}, f32[1,32,16,1]{3,2,1,0:T(8,128)S(1)}, u32[]{:S(2)}, u32[]{:S(2)}) collective-permute-start(f32[1,32,16,1]{3,2,1,0:T(8,128)S(1)} %get-tuple-element.47), channel_id=1, source_target_pairs={{32,0},{64,32},{96,64},{128,96},{160,128},{192,160},{224,192},{256... | collective-permute-start | bytes 6152 | tf_op jit(solution)/shard_map/ppermute | solution.py:23
  33.9 8.6 %collective-permute-start.5 = (f32[1,32,16,1]{3,2,1,0:T(8,128)S(1)}, f32[1,32,16,1]{3,2,1,0:T(8,128)S(1)}, u32[]{:S(2)}, u32[]{:S(2)}) collective-permute-start(f32[1,32,16,1]{3,2,1,0:T(8,128)S(1)} %get-tuple-element.45), channel_id=1, source_target_pairs={{32,0},{64,32},{96,64},{128,96},{160,128},{192,160},{224,192},{256... | collective-permute-start | bytes 6152 | tf_op jit(solution)/shard_map/ppermute | solution.py:23
  55.8 7.9 %collective-permute-start.8 = (f32[1,32,16,1]{3,2,1,0:T(8,128)S(1)}, f32[1,32,16,1]{3,2,1,0:T(8,128)S(1)}, u32[]{:S(2)}, u32[]{:S(2)}) collective-permute-start(f32[1,32,16,1]{3,2,1,0:T(8,128)S(1)} %get-tuple-element.42), channel_id=1, source_target_pairs={{0,32},{32,64},{64,96},{96,128},{128,160},{160,192},{192,224},{224... | collective-permute-start | bytes 6152 | tf_op jit(solution)/shard_map/ppermute | solution.py:22
  103.7 7.6 %collective-permute-start.16 = (f32[1,32,16,1]{3,2,1,0:T(8,128)S(1)}, f32[1,32,16,1]{3,2,1,0:T(8,128)S(1)}, u32[]{:S(2)}, u32[]{:S(2)}) collective-permute-start(f32[1,32,16,1]{3,2,1,0:T(8,128)S(1)} %get-tuple-element.38), channel_id=1, source_target_pairs={{0,32},{32,64},{64,96},{96,128},{128,160},{160,192},{192,224},{224... | collective-permute-start | bytes 6152 | tf_op jit(solution)/shard_map/ppermute | solution.py:22
  128.4 32.7 %collective-permute-start.20 = (f32[1,32,16,1]{3,2,1,0:T(8,128)}, f32[1,32,16,1]{3,2,1,0:T(8,128)}, u32[]{:S(2)}, u32[]{:S(2)}) collective-permute-start(f32[1,32,16,1]{3,2,1,0:T(8,128)} %get-tuple-element.36), channel_id=1, source_target_pairs={{0,32},{32,64},{64,96},{96,128},{128,160},{160,192},{192,224},{224... | collective-permute-start | bytes 6152 | tf_op jit(solution)/shard_map/ppermute | solution.py:22
  133.8 27.3 %collective-permute-start.21 = (f32[1,32,16,1]{3,2,1,0:T(8,128)}, f32[1,32,16,1]{3,2,1,0:T(8,128)}, u32[]{:S(2)}, u32[]{:S(2)}) collective-permute-start(f32[1,32,16,1]{3,2,1,0:T(8,128)} %get-tuple-element.37), channel_id=1, source_target_pairs={{32,0},{64,32},{96,64},{128,96},{160,128},{192,160},{224,192},{256... | collective-permute-start | bytes 6152 | tf_op jit(solution)/shard_map/ppermute | solution.py:23
  174.5 11.0 %collective-permute-start.24 = (f32[1,32,16,1]{3,2,1,0:T(8,128)S(1)}, f32[1,32,16,1]{3,2,1,0:T(8,128)S(1)}, u32[]{:S(2)}, u32[]{:S(2)}) collective-permute-start(f32[1,32,16,1]{3,2,1,0:T(8,128)S(1)} %get-tuple-element.34), channel_id=1, source_target_pairs={{0,32},{32,64},{64,96},{96,128},{128,160},{160,192},{192,224},{224... | collective-permute-start | bytes 6152 | tf_op jit(solution)/shard_map/ppermute | solution.py:22
  180.1 12.0 %collective-permute-start.32 = (f32[1,16,8,1]{3,2,1,0:T(8,128)S(1)}, f32[1,16,8,1]{3,2,1,0:T(8,128)S(1)}, u32[]{:S(2)}, u32[]{:S(2)}) collective-permute-start(f32[1,16,8,1]{3,2,1,0:T(8,128)S(1)} %get-tuple-element.84), channel_id=1, source_target_pairs={{0,32},{32,64},{64,96},{96,128},{128,160},{160,192},{192,224},{224... | collective-permute-start | bytes 1544 | tf_op jit(solution)/shard_map/ppermute | solution.py:22
  184.1 8.0 %collective-permute-start.33 = (f32[1,16,8,1]{3,2,1,0:T(8,128)S(1)}, f32[1,16,8,1]{3,2,1,0:T(8,128)S(1)}, u32[]{:S(2)}, u32[]{:S(2)}) collective-permute-start(f32[1,16,8,1]{3,2,1,0:T(8,128)S(1)} %get-tuple-element.85), channel_id=1, source_target_pairs={{32,0},{64,32},{96,64},{128,96},{160,128},{192,160},{224,192},{256... | collective-permute-start | bytes 1544 | tf_op jit(solution)/shard_map/ppermute | solution.py:23
  186.1 13.8 %collective-permute-start.26 = (f32[1,32,1,130]{3,2,1,0:T(1,128)S(1)}, f32[1,32,1,130]{3,2,1,0:T(1,128)S(1)}, u32[]{:S(2)}, u32[]{:S(2)}) collective-permute-start(f32[1,32,1,130]{3,2,1,0:T(1,128)S(1)} %get-tuple-element.14), channel_id=1, source_target_pairs={{0,1},{1,2},{2,3},{3,4},{4,5},{5,6},{6,7},{7,8},{8,9},{9,10},{10,1... | collective-permute-start | bytes 49928 | tf_op jit(solution)/shard_map/ppermute | solution.py:22
  190.2 9.8 %collective-permute-start.27 = (f32[1,32,1,130]{3,2,1,0:T(1,128)S(1)}, f32[1,32,1,130]{3,2,1,0:T(1,128)S(1)}, u32[]{:S(2)}, u32[]{:S(2)}) collective-permute-start(f32[1,32,1,130]{3,2,1,0:T(1,128)S(1)} %get-tuple-element.15), channel_id=1, source_target_pairs={{1,0},{2,1},{3,2},{4,3},{5,4},{6,5},{7,6},{8,7},{9,8},{10,9},{11,1... | collective-permute-start | bytes 49928 | tf_op jit(solution)/shard_map/ppermute | solution.py:23
  192.3 13.8 %collective-permute-start.34 = (f32[1,16,1,66]{3,2,1,0:T(1,128)S(1)}, f32[1,16,1,66]{3,2,1,0:T(1,128)S(1)}, u32[]{:S(2)}, u32[]{:S(2)}) collective-permute-start(f32[1,16,1,66]{3,2,1,0:T(1,128)S(1)} %get-tuple-element.64), channel_id=1, source_target_pairs={{0,1},{1,2},{2,3},{3,4},{4,5},{5,6},{6,7},{7,8},{8,9},{9,10},{10,1... | collective-permute-start | bytes 12680 | tf_op jit(solution)/shard_map/ppermute | solution.py:22
  198.0 8.0 %collective-permute-start.35 = (f32[1,16,1,66]{3,2,1,0:T(1,128)S(1)}, f32[1,16,1,66]{3,2,1,0:T(1,128)S(1)}, u32[]{:S(2)}, u32[]{:S(2)}) collective-permute-start(f32[1,16,1,66]{3,2,1,0:T(1,128)S(1)} %get-tuple-element.65), channel_id=1, source_target_pairs={{1,0},{2,1},{3,2},{4,3},{5,4},{6,5},{7,6},{8,7},{9,8},{10,9},{11,1... | collective-permute-start | bytes 12680 | tf_op jit(solution)/shard_map/ppermute | solution.py:23
  204.8 7.4 %collective-permute-start.29 = (f32[1,32,16,1]{3,2,1,0:T(8,128)S(1)}, f32[1,32,16,1]{3,2,1,0:T(8,128)S(1)}, u32[]{:S(2)}, u32[]{:S(2)}) collective-permute-start(f32[1,32,16,1]{3,2,1,0:T(8,128)S(1)} %get-tuple-element.33), channel_id=1, source_target_pairs={{32,0},{64,32},{96,64},{128,96},{160,128},{192,160},{224,192},{256... | collective-permute-start | bytes 6152 | tf_op jit(solution)/shard_map/ppermute | solution.py:23
  212.4 8.9 %collective-permute-start.30 = (f32[1,32,1,130]{3,2,1,0:T(1,128)S(1)}, f32[1,32,1,130]{3,2,1,0:T(1,128)S(1)}, u32[]{:S(2)}, u32[]{:S(2)}) collective-permute-start(f32[1,32,1,130]{3,2,1,0:T(1,128)S(1)} %get-tuple-element.12), channel_id=1, source_target_pairs={{0,1},{1,2},{2,3},{3,4},{4,5},{5,6},{6,7},{7,8},{8,9},{9,10},{10,1... | collective-permute-start | bytes 49928 | tf_op jit(solution)/shard_map/ppermute | solution.py:22
  232.1 7.5 %collective-permute-start.37 = (f32[1,32,16,1]{3,2,1,0:T(8,128)S(1)}, f32[1,32,16,1]{3,2,1,0:T(8,128)S(1)}, u32[]{:S(2)}, u32[]{:S(2)}) collective-permute-start(f32[1,32,16,1]{3,2,1,0:T(8,128)S(1)} %get-tuple-element.31), channel_id=1, source_target_pairs={{32,0},{64,32},{96,64},{128,96},{160,128},{192,160},{224,192},{256... | collective-permute-start | bytes 6152 | tf_op jit(solution)/shard_map/ppermute | solution.py:23
  375.9 9.9 %collective-permute-start.60 = (f32[1,16,8,1]{3,2,1,0:T(8,128)S(1)}, f32[1,16,8,1]{3,2,1,0:T(8,128)S(1)}, u32[]{:S(2)}, u32[]{:S(2)}) collective-permute-start(f32[1,16,8,1]{3,2,1,0:T(8,128)S(1)} %get-tuple-element.72), channel_id=1, source_target_pairs={{0,32},{32,64},{64,96},{96,128},{128,160},{160,192},{192,224},{224... | collective-permute-start | bytes 1544 | tf_op jit(solution)/shard_map/ppermute | solution.py:22
  380.6 10.2 %collective-permute-start.68 = (f32[1,8,4,1]{3,2,1,0:T(4,128)S(1)}, f32[1,8,4,1]{3,2,1,0:T(4,128)S(1)}, u32[]{:S(2)}, u32[]{:S(2)}) collective-permute-start(f32[1,8,4,1]{3,2,1,0:T(4,128)S(1)} %get-tuple-element.116), channel_id=1, source_target_pairs={{0,32},{32,64},{64,96},{96,128},{128,160},{160,192},{192,224},{224... | collective-permute-start | bytes 392 | tf_op jit(solution)/shard_map/ppermute | solution.py:22
  386.0 12.5 %collective-permute-start.62 = (f32[1,16,1,66]{3,2,1,0:T(1,128)S(1)}, f32[1,16,1,66]{3,2,1,0:T(1,128)S(1)}, u32[]{:S(2)}, u32[]{:S(2)}) collective-permute-start(f32[1,16,1,66]{3,2,1,0:T(1,128)S(1)} %get-tuple-element.52), channel_id=1, source_target_pairs={{0,1},{1,2},{2,3},{3,4},{4,5},{5,6},{6,7},{7,8},{8,9},{9,10},{10,1... | collective-permute-start | bytes 12680 | tf_op jit(solution)/shard_map/ppermute | solution.py:22
  388.8 9.8 %collective-permute-start.63 = (f32[1,16,1,66]{3,2,1,0:T(1,128)S(1)}, f32[1,16,1,66]{3,2,1,0:T(1,128)S(1)}, u32[]{:S(2)}, u32[]{:S(2)}) collective-permute-start(f32[1,16,1,66]{3,2,1,0:T(1,128)S(1)} %get-tuple-element.53), channel_id=1, source_target_pairs={{1,0},{2,1},{3,2},{4,3},{5,4},{6,5},{7,6},{8,7},{9,8},{10,9},{11,1... | collective-permute-start | bytes 12680 | tf_op jit(solution)/shard_map/ppermute | solution.py:23
  390.9 13.8 %collective-permute-start.70 = (f32[1,8,1,34]{3,2,1,0:T(1,128)S(1)}, f32[1,8,1,34]{3,2,1,0:T(1,128)S(1)}, u32[]{:S(2)}, u32[]{:S(2)}) collective-permute-start(f32[1,8,1,34]{3,2,1,0:T(1,128)S(1)} %get-tuple-element.100), channel_id=1, source_target_pairs={{0,1},{1,2},{2,3},{3,4},{4,5},{5,6},{6,7},{7,8},{8,9},{9,10},{10,1... | collective-permute-start | bytes 3272 | tf_op jit(solution)/shard_map/ppermute | solution.py:22
  396.6 8.0 %collective-permute-start.71 = (f32[1,8,1,34]{3,2,1,0:T(1,128)S(1)}, f32[1,8,1,34]{3,2,1,0:T(1,128)S(1)}, u32[]{:S(2)}, u32[]{:S(2)}) collective-permute-start(f32[1,8,1,34]{3,2,1,0:T(1,128)S(1)} %get-tuple-element.101), channel_id=1, source_target_pairs={{1,0},{2,1},{3,2},{4,3},{5,4},{6,5},{7,6},{8,7},{9,8},{10,9},{11,1... | collective-permute-start | bytes 3272 | tf_op jit(solution)/shard_map/ppermute | solution.py:23
  408.5 9.1 %collective-permute-start.66 = (f32[1,16,1,66]{3,2,1,0:T(1,128)S(1)}, f32[1,16,1,66]{3,2,1,0:T(1,128)S(1)}, u32[]{:S(2)}, u32[]{:S(2)}) collective-permute-start(f32[1,16,1,66]{3,2,1,0:T(1,128)S(1)} %get-tuple-element.50), channel_id=1, source_target_pairs={{0,1},{1,2},{2,3},{3,4},{4,5},{5,6},{6,7},{7,8},{8,9},{9,10},{10,1... | collective-permute-start | bytes 12680 | tf_op jit(solution)/shard_map/ppermute | solution.py:22
  (82 other events, 644.1 us)
where the time goes:
time: 579 us; the launch traced here: 575 us
  starting transfers between devices  280 us (48%)
  waiting for transfers between devices  206 us (36%)
  local copies, waits for them, and re-layouts  45.2 us (8%)
  other arithmetic  42.5 us (7%)
    ppermute x52, starting transfers between devices, padded(): before = lax.ppermute(last, axis, up)  195 us
    ppermute x52, waiting for transfers between devices, padded(): after = lax.ppermute(leading, axis, down)  190 us
    ppermute x52, starting transfers between devices, padded(): after = lax.ppermute(leading, axis, down)  84.4 us
    reshape x3, local copies, waits for them, and re-layouts, restrict(): cells.reshape(depth_cells // 2, 2, row_cells // 2, 2, column_cells // 2, 2)  39.8 us
    ppermute x52, waiting for transfers between devices, padded(): before = lax.ppermute(last, axis, up)  15.5 us
    reduce_sum x4, other arithmetic, restrict(): cells.reshape(depth_cells // 2, 2, row_cells // 2, 2, column_cells // 2, 2)  14.5 us
  transfers between devices with their start and end apart: 104, of which 51 were waited for; matrix products, arithmetic and copies ran while one was open for 5% of the time, Pallas kernels for 0%

commit v1 on v0

v1 whole, which is shorter than its diff:
```python
import functools

import jax
import jax.numpy as jnp
from jax import lax
from jax.experimental import pallas as pl
from jax.experimental.pallas import tpu as pltpu
from jax.sharding import PartitionSpec as P

MESH = pl.DeviceIdType.MESH
F32 = jnp.float32
STORAGE = 0.05
LEAK = 0.1
TINY = 1e-30

HALO = 9
ROWS = 16 + 2 * HALO
MID = 24
LOW = 20
MX = 22
LX = 11


def rcp(d):
    r = pl.reciprocal(d, approx=True)
    return r * (2.0 - d * r)


def harm(a, b):
    return (2.0 * a * b) * rcp(jnp.maximum(a + b, TINY))


def lane_of(shape):
    return lax.broadcasted_iota(jnp.int32, shape, len(shape) - 1)


def sub_of(shape):
    return lax.broadcasted_iota(jnp.int32, shape, len(shape) - 2)


def roll(x, shift):
    shift = shift % 128
    return x if shift == 0 else pltpu.roll(x, shift, x.ndim - 1)


def east(x):
    return roll(x, 127)


def west(x):
    return roll(x, 1)


def up(x):
    return pltpu.roll(x, 7, x.ndim - 2)


def down(x):
    return pltpu.roll(x, 1, x.ndim - 2)


def strip_up(x):
    y = roll(x, 96)
    return jnp.where(lane_of(x.shape) >= 96, up(y), y)


def strip_down(x):
    y = roll(x, 32)
    return jnp.where(lane_of(x.shape) < 32, down(y), y)


def groups(parts, shifts):
    lane = lane_of(parts[0].shape)
    out = roll(parts[3], shifts[3])
    for q in (2, 1, 0):
        out = jnp.where(lane < 32 * (q + 1), roll(parts[q], shifts[q]), out)
    return out


def pack_west(m):
    return groups(m, [32 * k + 9 for k in range(4)])


def pack_east(m):
    return groups(m, [32 * k + 23 for k in range(4)])


def main_east(m, k, strip):
    ins = roll(strip, 104 - 32 * k)
    return jnp.where(lane_of(m.shape) == 127, ins, east(m))


def main_west(m, k, strip):
    ins = roll(strip, -(32 * k + 8))
    return jnp.where(lane_of(m.shape) == 0, ins, west(m))


def finish(t, c, store):
    total = t[0]
    for x in t[1:]:
        total = total + x
    return total + store * c + jnp.where(c > 0.0, 0.0, 1.0)


def kernel(ngx, ngy, perm, source, mask, out_fine, out_mid, out_low,
           cm, bm, sr, sl, rl, rr, cs, cse, csw, coef, inv, v,
           cmx, cmid, midx, mrl, mrr, mcoef, mvx, mv, clow, lcoef, lvx, lv, tmid, tlow, send, recv):
    gx, gy = lax.axis_index("gx"), lax.axis_index("gy")

    def dev(dx, dy):
        return (lax.rem(gx + dx + ngx, ngx), lax.rem(gy + dy + 2 * ngy, ngy))

    around = [(dx, dy) for dx in (-1, 0, 1) for dy in (-1, 0, 1) if (dx, dy) != (0, 0)]
    partners = around + [(0, -2), (0, 2)]
    barrier = pltpu.get_barrier_semaphore()
    for d in partners:
        pl.semaphore_signal(barrier, inc=1, device_id=dev(*d), device_id_type=MESH)

    made = [0]

    def copy(src, dst, to):
        i = made[0]
        made[0] += 1
        return pltpu.make_async_remote_copy(
            src_ref=src, dst_ref=dst, send_sem=send.at[i], recv_sem=recv.at[i],
            device_id=dev(*to), device_id_type=MESH)


    def take(ref, y, k):
        return ref[pl.ds(k * 16 + y, 8, stride=64), :]

    lane = lane_of((8, 128))
    sub = sub_of((8, 128))
    pair_mid = jnp.clip(2 * (lane - MX), 0, 127)
    pair_low = jnp.clip(2 * lane, 0, 127)

    def compact(x, index):
        return jnp.take_along_axis(x + east(x), index, axis=1, mode="promise_in_bounds")

    def load_pair(i, carry):
        acc = [None, None]
        for o in range(2):
            y = 2 * i + o
            conds, rights = [], []
            for k in range(4):
                p, m = take(perm, y, k), take(mask, y, k)
                c = jnp.where(m == 2, 0.0, p)
                b = jnp.where(m == 1, take(source, y, k), 0.0)
                cm[HALO + y, k] = c
                bm[HALO + y, k] = b
                conds.append(c)
                rights.append(b)
                term = LEAK * p + (1.0 - LEAK) * c
                acc[k // 2] = term if acc[k // 2] is None else acc[k // 2] + term
            aw, ae = pack_west(conds), pack_east(conds)
            bw, be = pack_west(rights), pack_east(rights)
            c32 = jnp.bitwise_and(lane, 31)
            sr[y] = jnp.where(c32 < 16, aw, roll(bw, 16))
            sl[y] = jnp.where(c32 >= 16, ae, roll(be, 112))
        for k in range(2):
            cmx[8 + i, k] = compact(acc[k], pair_mid) * 0.125
        return carry

    lax.fori_loop(0, 8, load_pair, 0)

    def mid_pack(src, row0, slot):
        for i in range(4):
            parts = [src[row0 + i + 4 * (q // 2), q % 2] for q in range(4)]
            midx[slot, 0, i] = groups(parts, [32 * q - (MX + 42) for q in range(4)])
            midx[slot, 1, i] = groups(parts, [32 * q - MX for q in range(4)])

    mid_pack(cmx, 8, 0)
    pl.semaphore_wait(barrier, len(partners))

    def start(cs_):
        for c_ in cs_:
            c_.start()

    def arrive(cs_):
        for c_ in cs_:
            c_.wait_recv()

    def strips(src_r, src_l, dst_l, dst_r, n):
        own = src_r.shape[0]
        got = []
        for dx, src, dst in ((1, src_r, dst_l), (-1, src_l, dst_r)):
            got.append(copy(src, dst.at[pl.ds(n, own)], (dx, 0)))
            got.append(copy(src.at[pl.ds(own - n, n)], dst.at[pl.ds(0, n)], (dx, 1)))
            got.append(copy(src.at[pl.ds(0, n)], dst.at[pl.ds(n + own, n)], (dx, -1)))
        return got

    def edges(buf, n, own, first=0):
        return [copy(buf.at[pl.ds(first + own, n)], buf.at[pl.ds(first, n)], (0, 1)),
                copy(buf.at[pl.ds(first + n, n)], buf.at[pl.ds(first + n + own, n)], (0, -1))]

    cond_y = edges(cm, HALO, 16)
    raw_x = strips(sr, sl, rl, rr, HALO)
    right_y = edges(bm, HALO, 16)
    start(cond_y + raw_x + right_y)

    def mid_exchange(buf, slot):
        got = edges(buf, 8, 8)
        for dx, side, dst in ((1, 0, mrl), (-1, 1, mrr)):
            src = midx.at[slot, side]
            for dy, block in ((0, 1), (1, 0), (-1, 2)):
                got.append(copy(src, dst.at[slot, block], (dx, dy)))
        return got

    cond_mid = mid_exchange(cmx, 0)
    start(cond_mid)

    arrive(cond_y + raw_x)

    @pl.when(gy == 0)
    def _():
        cm[pl.ds(0, HALO)] = jnp.zeros((HALO, 4, 8, 128), F32)

    @pl.when(gy == ngy - 1)
    def _():
        cm[pl.ds(16 + HALO, HALO)] = jnp.zeros((HALO, 4, 8, 128), F32)

    c32 = jnp.bitwise_and(lane, 31)
    inside = jnp.where(gx == 0, 9, 0), jnp.where(gx == ngx - 1, 23, 32)
    keep = (c32 >= inside[0]) & (c32 < inside[1])

    def strip_row(r, carry):
        parts = [cm[r, k] for k in range(4)]
        aw, ae = pack_west(parts), pack_east(parts)
        live = jnp.where(((gy == 0) & (r < HALO)) | ((gy == ngy - 1) & (r >= HALO + 16)), 0.0, 1.0)
        c = jnp.where(c32 < 9, rl[r], jnp.where(c32 < 16, aw, jnp.where(c32 < 23, ae, rr[r])))
        c = jnp.where(keep, c, 0.0) * live
        cs[r] = c
        cse[r] = east(jnp.where(c32 == 16, aw, c))
        csw[r] = west(jnp.where(c32 == 15, ae, c))
        return carry

    lax.fori_loop(0, ROWS, strip_row, 0, unroll=2)

    top = sub == 7

    def fine_coefs(i, carry):
        r = 1 + i
        m = [[cm[r + d, k] for k in range(4)] for d in (-1, 0, 1)]
        s = [cs[r + d] for d in (-1, 0, 1)]
        se = cse[r]
        c = s[1]
        te = harm(c, se)
        tw = harm(c, csw[r])
        tn, ts = harm(c, s[2]), harm(c, s[0])
        tu = harm(c, jnp.where(top & (lane >= 96), 0.0, strip_up(c)))
        faces = [te, tw, tn, ts, tu, strip_down(tu)]

        def put(k, faces, c):
            diag = finish(faces, c, STORAGE)
            w = 0.8 * rcp(diag)
            for f in range(6):
                coef[f, r, k] = w * faces[f]
            coef[6, r, k] = w
            inv[r, k] = 1.25 * diag

        put(4, faces, c)
        ups = [harm(m[1][k], m[1][k + 1]) for k in range(3)]
        ups.append(harm(m[1][3], jnp.where(top, 0.0, up(m[1][0]))))
        for k in range(4):
            c = m[1][k]
            e = harm(c, main_east(c, k, s[1]))
            w_ = main_west(e, k, te)
            d_ = ups[k - 1] if k else down(ups[3])
            put(k, [e, w_, harm(c, m[2][k]), harm(c, m[0][k]), ups[k], d_], c)
        return carry

    lax.fori_loop(0, ROWS - 2, fine_coefs, 0, unroll=2)

    arrive(right_y)
    for p in range(2):
        for r in (0, ROWS - 1):
            v[p, r] = jnp.zeros((5, 8, 128), F32)

    def first(i, carry):
        r = 1 + i
        parts = [bm[r, k] for k in range(4)]
        for k in range(4):
            v[0, r, k] = coef[6, r, k] * parts[k]
        aw, ae = pack_west(parts), pack_east(parts)
        b = jnp.where(c32 < 9, roll(rl[r], 112), jnp.where(c32 < 16, aw, jnp.where(c32 < 23, ae, roll(rr[r], 16))))
        x = coef[6, r, 4] * b
        v[0, r, 4] = x
        coef[6, r, 4] = x
        for k in range(4):
            coef[6, r, k] = v[0, r, k]
        return carry

    lax.fori_loop(0, ROWS - 2, first, 0, unroll=2)

    def sweep_main(p, r, k, x, x0, x2, strip):
        u = x[k + 1] if k < 3 else up(x[0])
        d = x[k - 1] if k else down(x[3])
        a = [coef[f, r, k] for f in range(7)]
        return (0.2 * x[k] + a[6] + a[0] * main_east(x[k], k, strip) + a[1] * main_west(x[k], k, strip)
                + a[2] * x2[k] + a[3] * x0[k] + a[4] * u + a[5] * d)

    def sweep(j, carry):
        p, half = lax.rem(j + 1, 2), lax.div(j, 2)
        q = 1 - p

        def block(i, carry):
            r0 = 1 + 2 * half + 4 * i
            rows = [[v[p, r0 + o - 1, k] for k in range(5)] for o in range(6)]
            for o in range(4):
                x0, x, x2 = rows[o], rows[o + 1], rows[o + 2]
                r = r0 + o
                new = []
                for k in range(4):
                    new.append(sweep_main(p, r, k, x, x0, x2, x[4]))
                s = x[4]
                a = [coef[f, r, 4] for f in range(7)]
                new.append(0.2 * s + a[6] + a[0] * east(s) + a[1] * west(s) + a[2] * x2[4] + a[3] * x0[4]
                           + a[4] * strip_up(s) + a[5] * strip_down(s))
                for k in range(5):
                    v[q, r, k] = new[k]
            return carry

        lax.fori_loop(0, 8 - half, block, 0)
        return carry

    lax.fori_loop(1, 8, sweep, 0)

    def mid_join(buf, slot, row):
        block, i = row // 8, row % 8
        out = []
        for k in range(2):
            q = 2 * (i // 4) + k
            left = roll(mrl[slot, block, i % 4], -32 * q)
            right = roll(mrr[slot, block, i % 4], MX + 64 - 32 * q)
            out.append(jnp.where(lane < MX, left, jnp.where(lane < MX + 64, buf[row, k], right)))
        return out

    arrive(cond_mid)
    lo, hi = jnp.where(gx == 0, MX, 0), jnp.where(gx == ngx - 1, MX + 64, 128)
    keep_mid = (lane >= lo) & (lane < hi)
    live = [jnp.where(gy == 0, 0.0, 1.0), 1.0, jnp.where(gy == ngy - 1, 0.0, 1.0)]
    for row in range(MID):
        joined = mid_join(cmx, 0, row)
        for k in range(2):
            c = jnp.where(keep_mid, joined[k], 0.0)
            cmid[row, k] = c if row // 8 == 1 else c * live[row // 8]

    def mid_coefs(i, carry):
        r = 1 + i
        x = [[cmid[r + d, k] for k in range(2)] for d in (-1, 0, 1)]
        u = [2.0 * harm(x[1][0], x[1][1]), 2.0 * harm(x[1][1], jnp.where(top, 0.0, up(x[1][0])))]
        for k in range(2):
            c = x[1][k]
            e = 2.0 * harm(c, east(c))
            faces = [e, west(e), 2.0 * harm(c, x[2][k]), 2.0 * harm(c, x[0][k]), u[k], u[0] if k else down(u[1])]
            diag = finish(faces, c, 8.0 * STORAGE)
            w = 0.8 * rcp(diag)
            for f in range(6):
                mcoef[f, r, k] = w * faces[f]
            mcoef[6, r, k] = w
            mcoef[7, r, k] = 1.25 * diag
        return carry

    lax.fori_loop(0, MID - 2, mid_coefs, 0, unroll=2)

    for i in range(4):
        acc = cmid[8 + 2 * i, 0] + cmid[8 + 2 * i, 1] + cmid[9 + 2 * i, 0] + cmid[9 + 2 * i, 1]
        clow[8 + i] = compact(acc, pair_low) * 0.125

    def low_exchange(buf):
        return [copy(buf.at[pl.ds(8, 4)], buf.at[pl.ds(4, 4)], (0, 1)),
                copy(buf.at[pl.ds(8, 4)], buf.at[pl.ds(12, 4)], (0, -1)),
                copy(buf.at[pl.ds(8, 4)], buf.at[pl.ds(0, 4)], (0, 2)),
                copy(buf.at[pl.ds(8, 4)], buf.at[pl.ds(16, 4)], (0, -2))]

    cond_low = low_exchange(clow)
    start(cond_low)

    def fine_residual(i, carry):
        acc = [None, None]
        r0 = HALO + 2 * i
        rows = [[v[1, r0 + o - 1, k] for k in range(4)] for o in range(4)]
        for o in range(2):
            r = r0 + o
            x0, x, x2 = rows[o], rows[o + 1], rows[o + 2]
            strip = v[1, r, 4]
            for k in range(4):
                res = (sweep_main(1, r, k, x, x0, x2, strip) - x[k]) * inv[r, k]
                acc[k // 2] = res if acc[k // 2] is None else acc[k // 2] + res
        for k in range(2):
            mvx[8 + i, k] = mcoef[6, 8 + i, k] * compact(acc[k], pair_mid)
        return carry

    lax.fori_loop(0, 8, fine_residual, 0)
    mid_pack(mvx, 8, 1)
    right_mid = mid_exchange(mvx, 1)
    start(right_mid)

    def write_fine(y, carry):
        for k in range(4):
            out_fine[pl.ds(k * 16 + y, 8, stride=64), :] = v[1, HALO + y, k]
        return carry

    lax.fori_loop(0, 16, write_fine, 0, unroll=4)

    arrive(cond_low)
    for row in list(range(1, 8)) + list(range(12, 19)):
        far = ngy - 1 - gy if row >= 12 else gy
        near = (row - 12) // 4 + 1 if row >= 12 else (11 - row) // 4
        clow[row] = clow[row] * jnp.where(far < near, 0.0, 1.0)

    for r in range(2, 18):
        c = clow[r]
        u = 4.0 * harm(c, jnp.where(top, 0.0, up(c)))
        e = 4.0 * harm(c, east(c))
        faces = [e, west(e), 4.0 * harm(c, clow[r + 1]), 4.0 * harm(c, clow[r - 1]), u, down(u)]
        diag = finish(faces, c, 64.0 * STORAGE)
        w = 0.8 * rcp(diag)
        for f in range(6):
            lcoef[f, r] = w * faces[f]
        lcoef[6, r] = w

    arrive(right_mid)
    for row in range(MID):
        joined = mid_join(mvx, 1, row)
        for k in range(2):
            mv[0, row, k] = joined[k]
            mcoef[6, row, k] = joined[k]

    def mid_sweep(p, r):
        x0, x, x2 = ([mv[p, r + d, k] for k in range(2)] for d in (-1, 0, 1))
        out = []
        for k in range(2):
            a = [mcoef[f, r, k] for f in range(7)]
            u = x[1] if k == 0 else up(x[0])
            d = x[0] if k else down(x[1])
            out.append(0.2 * x[k] + a[6] + a[0] * east(x[k]) + a[1] * west(x[k]) + a[2] * x2[k] + a[3] * x0[k]
                       + a[4] * u + a[5] * d)
        return x, out

    for j in range(1, 8):
        p, q = (j + 1) % 2, j % 2
        for r in range(j, MID - j):
            _, new = mid_sweep(p, r)
            for k in range(2):
                mv[q, r, k] = new[k]

    for i in range(4):
        acc = None
        for o in range(2):
            r = 8 + 2 * i + o
            x, new = mid_sweep(1, r)
            for k in range(2):
                res = (new[k] - x[k]) * mcoef[7, r, k]
                acc = res if acc is None else acc + res
        lvx[8 + i] = lcoef[6, 8 + i] * compact(acc, pair_low)
    right_low = low_exchange(lvx)
    start(right_low)

    for i in range(8):
        for k in range(2):
            tmid[pl.ds(k * 8 + i, 8, stride=16), :] = roll(mv[1, 8 + i, k], -MX)
    out_mid[...] = tmid[...].reshape(16, 8, 128)[:, :, :64]

    arrive(right_low)
    for j in range(1, 8):
        src, q = lvx if j == 1 else lv.at[(j + 1) % 2], j % 2
        for r in range(1 + j, LOW - 1 - j):
            x = src[r]
            a = [lcoef[f, r] for f in range(6)]
            lv[q, r] = (0.2 * x + lvx[r] + a[0] * east(x) + a[1] * west(x) + a[2] * src[r + 1] + a[3] * src[r - 1]
                        + a[4] * up(x) + a[5] * down(x))
    for i in range(4):
        tlow[pl.ds(i, 8, stride=8), :] = roll(lv[1, 8 + i], -LX)
    out_low[...] = tlow[...].reshape(8, 8, 128)[:, :4, :32]

    for c_ in cond_y + raw_x + right_y + cond_mid + cond_low + right_mid + right_low:
        c_.wait_send()


N_COPIES = 2 + 6 + 2 + 8 + 4 + 8 + 4


def per_device(ngx, ngy, permeability, source, phase_mask):
    vmem = pl.BlockSpec(memory_space=pltpu.VMEM)
    vec = lambda *dims: pltpu.VMEM(dims + (8, 128), F32)
    flat = [x.reshape(512, 128) for x in (permeability, source, phase_mask)]
    fine, mid, low = pl.pallas_call(
        functools.partial(kernel, ngx, ngy),
        out_shape=(
            jax.ShapeDtypeStruct((512, 128), F32),
            jax.ShapeDtypeStruct((16, 8, 64), F32),
            jax.ShapeDtypeStruct((8, 4, 32), F32),
        ),
        in_specs=[vmem] * 3,
        out_specs=(vmem,) * 3,
        scratch_shapes=[
            vec(ROWS, 4), vec(ROWS, 4),
            vec(16), vec(16), vec(ROWS), vec(ROWS),
            vec(ROWS), vec(ROWS), vec(ROWS),
            vec(7, ROWS, 5), vec(ROWS, 5), vec(2, ROWS, 5),
            vec(MID, 2), vec(MID, 2), vec(2, 2, 4), vec(2, 3, 4), vec(2, 3, 4),
            vec(8, MID, 2), vec(MID, 2), vec(2, MID, 2),
            vec(LOW), vec(7, LOW), vec(LOW), vec(2, LOW),
            pltpu.VMEM((128, 128), F32), pltpu.VMEM((64, 128), F32),
            pltpu.SemaphoreType.DMA((N_COPIES,)), pltpu.SemaphoreType.DMA((N_COPIES,)),
        ],
        compiler_params=pltpu.CompilerParams(
            collective_id=0, has_side_effects=True, vmem_limit_bytes=40 * 2**20),
    )(*flat)
    return fine.reshape(32, 16, 128), mid, low


def solution(mesh):
    placed = (P(None, "gy", "gx"),) * 3
    return jax.shard_map(
        functools.partial(per_device, mesh.shape["gx"], mesh.shape["gy"]),
        mesh=mesh, in_specs=placed, out_specs=placed, check_vma=False)
```

time: 579 us -> 56.3 us (0.10)
  the two profiles are of different devices: /device:TPU:7 before, /device:TPU:1 now
where the time goes in v1:
time: 56.3 us; the launch traced here: 56.1 us
  Pallas kernels  50.6 us (90%)
  local copies, waits for them, and re-layouts  4.78 us (8%)
  between operations  0.65 us (1%)
    pallas_call x1, Pallas kernels, per_device(): pl.pallas_call(functools.partial(kernel, ngx, ngy), out_shape=(jax.ShapeD...  50.6 us
    unnamed x9, local copies, waits for them, and re-layouts  4.78 us

profile of v1, /device:TPU:1, one launch (start us, length us, event | category | flops | bytes accessed | tf_op | source)
XLA Modules:
  0.0 56.1 jit_solution(8117517772232412593)
XLA Ops:
  0.6 0.0 copy-start
  0.6 0.9 %copy-done = f32[32,16,128]{2,1,0:T(8,128)S(1)} copy-done((f32[32,16,128]{2,1,0:T(8,128)S(1)}, f32[32,16,128]{2,1,0:T(8,128)}, u32[]{:S(2)}) %copy-start) | copy-done | bytes 262168
  1.6 0.0 copy-start.1
  1.6 0.9 %copy-done.1 = f32[32,16,128]{2,1,0:T(8,128)S(1)} copy-done((f32[32,16,128]{2,1,0:T(8,128)S(1)}, f32[32,16,128]{2,1,0:T(8,128)}, u32[]{:S(2)}) %copy-start.1) | copy-done | bytes 262168
  2.5 0.0 copy-start.2
  2.5 0.9 %copy-done.2 = s32[32,16,128]{2,1,0:T(8,128)S(1)} copy-done((s32[32,16,128]{2,1,0:T(8,128)S(1)}, s32[32,16,128]{2,1,0:T(8,128)}, u32[]{:S(2)}) %copy-start.2) | copy-done | bytes 262168
  3.5 50.6 %shard_map.58 = (f32[512,128]{1,0:T(8,128)S(1)}, f32[16,8,64]{2,1,0:T(8,128)S(1)}, f32[8,4,32]{2,1,0:T(4,128)S(1)}) custom-call(f32[512,128]{1,0:T(8,128)S(1)} %bitcast.4, f32[512,128]{1,0:T(8,128)S(1)} %bitcast.5, s32[512,128]{1,0:T(8,128)S(1)} %bitcast.6), custom_call_target="tpu_custom_call" | custom-call | tf_op jit(solution)/shard_map/pallas_call | solution.py:488
  54.1 0.7 %copy.9 = f32[32,16,128]{2,1,0:T(8,128)} copy(f32[32,16,128]{2,1,0:T(8,128)S(1)} %bitcast.7) | data formatting | bytes 524288
  54.8 0.6 %copy.10 = f32[16,8,64]{2,1,0:T(8,128)} copy(f32[16,8,64]{2,1,0:T(8,128)S(1)} %get-tuple-element.13) | data formatting | bytes 65536
  55.5 0.6 %copy.11 = f32[8,4,32]{2,1,0:T(4,128)} copy(f32[8,4,32]{2,1,0:T(4,128)S(1)} %get-tuple-element.14) | data formatting | bytes 8192
Async XLA Ops:
  0.6 1.0 %copy-start = (f32[32,16,128]{2,1,0:T(8,128)S(1)}, f32[32,16,128]{2,1,0:T(8,128)}, u32[]{:S(2)}) copy-start(f32[32,16,128]{2,1,0:T(8,128)} %param.3) | copy-start | bytes 786436
  1.6 0.9 %copy-start.1 = (f32[32,16,128]{2,1,0:T(8,128)S(1)}, f32[32,16,128]{2,1,0:T(8,128)}, u32[]{:S(2)}) copy-start(f32[32,16,128]{2,1,0:T(8,128)} %param.4) | copy-start | bytes 786436
  2.5 0.9 %copy-start.2 = (s32[32,16,128]{2,1,0:T(8,128)S(1)}, s32[32,16,128]{2,1,0:T(8,128)}, u32[]{:S(2)}) copy-start(s32[32,16,128]{2,1,0:T(8,128)} %param.5) | copy-start | bytes 786436

commit v2 on v1

--- a/solution.py
+++ b/solution.py
@@ -102,18 +102,21 @@
     return total + store * c + jnp.where(c > 0.0, 0.0, 1.0)
 
 
-def kernel(ngx, ngy, perm, source, mask, out_fine, out_mid, out_low,
-           cm, bm, sr, sl, rl, rr, cs, cse, csw, coef, inv, v,
-           cmx, cmid, midx, mrl, mrr, mcoef, mvx, mv, clow, lcoef, lvx, lv, tmid, tlow, send, recv):
+def kernel(ngx, ngy, perm_in, source_in, mask_in, out_fine, out_mid, out_low,
+           cm, bm, own_w, own_e, own_b, sr, sl, rl, rr, cs, cse, csw, coef, inv, v,
+           cmx, cmid, midx, mrl, mrr, mcoef, mvx, mv, clow, lcoef, lvx, lv, tmid, tlow, perm, source, mask, send, recv, load):
     gx, gy = lax.axis_index("gx"), lax.axis_index("gy")
+    loads = [pltpu.make_async_copy(a, b, load.at[i])
+             for i, (a, b) in enumerate(((perm_in, perm), (mask_in, mask), (source_in, source)))]
+    for l in loads:
+        l.start()
 
     def dev(dx, dy):
         return (lax.rem(gx + dx + ngx, ngx), lax.rem(gy + dy + 2 * ngy, ngy))
 
     around = [(dx, dy) for dx in (-1, 0, 1) for dy in (-1, 0, 1) if (dx, dy) != (0, 0)]
-    partners = around + [(0, -2), (0, 2)]
     barrier = pltpu.get_barrier_semaphore()
-    for d in partners:
+    for d in around:
         pl.semaphore_signal(barrier, inc=1, device_id=dev(*d), device_id_type=MESH)
 
     made = [0]
@@ -130,12 +133,16 @@
         return ref[pl.ds(k * 16 + y, 8, stride=64), :]
 
     lane = lane_of((8, 128))
+    c32 = jnp.bitwise_and(lane, 31)
     sub = sub_of((8, 128))
     pair_mid = jnp.clip(2 * (lane - MX), 0, 127)
     pair_low = jnp.clip(2 * lane, 0, 127)
 
     def compact(x, index):
         return jnp.take_along_axis(x + east(x), index, axis=1, mode="promise_in_bounds")
+
+    for l in loads:
+        l.wait()
 
     def load_pair(i, carry):
         acc = [None, None]
@@ -154,14 +161,15 @@
                 acc[k // 2] = term if acc[k // 2] is None else acc[k // 2] + term
             aw, ae = pack_west(conds), pack_east(conds)
             bw, be = pack_west(rights), pack_east(rights)
-            c32 = jnp.bitwise_and(lane, 31)
+            own_w[y], own_e[y] = aw, ae
+            own_b[y] = jnp.where(c32 < 16, bw, be)
             sr[y] = jnp.where(c32 < 16, aw, roll(bw, 16))
             sl[y] = jnp.where(c32 >= 16, ae, roll(be, 112))
         for k in range(2):
             cmx[8 + i, k] = compact(acc[k], pair_mid) * 0.125
         return carry
 
-    lax.fori_loop(0, 8, load_pair, 0)
+    lax.fori_loop(0, 8, load_pair, 0, unroll=True)
 
     def mid_pack(src, row0, slot):
         for i in range(4):
@@ -170,7 +178,7 @@
             midx[slot, 1, i] = groups(parts, [32 * q - MX for q in range(4)])
 
     mid_pack(cmx, 8, 0)
-    pl.semaphore_wait(barrier, len(partners))
+    pl.semaphore_wait(barrier, len(around))
 
     def start(cs_):
         for c_ in cs_:
@@ -209,37 +217,21 @@
     cond_mid = mid_exchange(cmx, 0)
     start(cond_mid)
 
-    arrive(cond_y + raw_x)
-
-    @pl.when(gy == 0)
-    def _():
-        cm[pl.ds(0, HALO)] = jnp.zeros((HALO, 4, 8, 128), F32)
-
-    @pl.when(gy == ngy - 1)
-    def _():
-        cm[pl.ds(16 + HALO, HALO)] = jnp.zeros((HALO, 4, 8, 128), F32)
-
-    c32 = jnp.bitwise_and(lane, 31)
     inside = jnp.where(gx == 0, 9, 0), jnp.where(gx == ngx - 1, 23, 32)
     keep = (c32 >= inside[0]) & (c32 < inside[1])
 
-    def strip_row(r, carry):
-        parts = [cm[r, k] for k in range(4)]
-        aw, ae = pack_west(parts), pack_east(parts)
-        live = jnp.where(((gy == 0) & (r < HALO)) | ((gy == ngy - 1) & (r >= HALO + 16)), 0.0, 1.0)
+    def strip_cond(r, aw, ae, live=None):
         c = jnp.where(c32 < 9, rl[r], jnp.where(c32 < 16, aw, jnp.where(c32 < 23, ae, rr[r])))
-        c = jnp.where(keep, c, 0.0) * live
+        c = jnp.where(keep, c, 0.0)
+        if live is not None:
+            c = c * live
         cs[r] = c
         cse[r] = east(jnp.where(c32 == 16, aw, c))
         csw[r] = west(jnp.where(c32 == 15, ae, c))
-        return carry
-
-    lax.fori_loop(0, ROWS, strip_row, 0, unroll=2)
 
     top = sub == 7
 
-    def fine_coefs(i, carry):
-        r = 1 + i
+    def fine_coefs(r):
         m = [[cm[r + d, k] for k in range(4)] for d in (-1, 0, 1)]
         s = [cs[r + d] for d in (-1, 0, 1)]
         se = cse[r]
@@ -267,63 +259,97 @@
             w_ = main_west(e, k, te)
             d_ = ups[k - 1] if k else down(ups[3])
             put(k, [e, w_, harm(c, m[2][k]), harm(c, m[0][k]), ups[k], d_], c)
-        return carry
-
-    lax.fori_loop(0, ROWS - 2, fine_coefs, 0, unroll=2)
+
+    def first(r, mid):
+        b = [bm[r, k] for k in range(4)]
+        b.append(jnp.where(c32 < 9, roll(rl[r], 112), jnp.where(c32 < 23, mid, roll(rr[r], 16))))
+        for k in range(5):
+            x = coef[6, r, k] * b[k]
+            v[r, k] = x
+            coef[6, r, k] = x
+
+    def loop(n, unroll):
+        def run(body):
+            def step(i, carry):
+                body(i)
+                return carry
+            lax.fori_loop(0, n, step, 0, unroll=unroll)
+        return run
+
+    arrive([raw_x[0], raw_x[3]])
+
+    @loop(16, True)
+    def _(i):
+        strip_cond(HALO + i, own_w[i], own_e[i])
+
+    @loop(14, 7)
+    def _(i):
+        fine_coefs(HALO + 1 + i)
+
+    @loop(14, 7)
+    def _(i):
+        first(HALO + 1 + i, own_b[1 + i])
+
+    arrive(cond_y + raw_x[1:3] + raw_x[4:6])
+
+    @pl.when(gy == 0)
+    def _():
+        cm[pl.ds(0, HALO)] = jnp.zeros((HALO, 4, 8, 128), F32)
+
+    @pl.when(gy == ngy - 1)
+    def _():
+        cm[pl.ds(16 + HALO, HALO)] = jnp.zeros((HALO, 4, 8, 128), F32)
+
+    lives = [jnp.where(gy == 0, 0.0, 1.0), jnp.where(gy == ngy - 1, 0.0, 1.0)]
+
+    @loop(HALO, True)
+    def _(i):
+        for r, live in ((i, lives[0]), (16 + HALO + i, lives[1])):
+            parts = [cm[r, k] for k in range(4)]
+            strip_cond(r, pack_west(parts), pack_east(parts), live)
+
+    @loop(HALO, 3)
+    def _(i):
+        for r in (1 + i, 15 + HALO + i):
+            fine_coefs(r)
 
     arrive(right_y)
-    for p in range(2):
-        for r in (0, ROWS - 1):
-            v[p, r] = jnp.zeros((5, 8, 128), F32)
-
-    def first(i, carry):
-        r = 1 + i
-        parts = [bm[r, k] for k in range(4)]
-        for k in range(4):
-            v[0, r, k] = coef[6, r, k] * parts[k]
-        aw, ae = pack_west(parts), pack_east(parts)
-        b = jnp.where(c32 < 9, roll(rl[r], 112), jnp.where(c32 < 16, aw, jnp.where(c32 < 23, ae, roll(rr[r], 16))))
-        x = coef[6, r, 4] * b
-        v[0, r, 4] = x
-        coef[6, r, 4] = x
-        for k in range(4):
-            coef[6, r, k] = v[0, r, k]
-        return carry
-
-    lax.fori_loop(0, ROWS - 2, first, 0, unroll=2)
-
-    def sweep_main(p, r, k, x, x0, x2, strip):
+    first(HALO, own_b[0])
+    first(HALO + 15, own_b[15])
+
+    @loop(HALO - 1, 4)
+    def _(i):
+        for r in (1 + i, 16 + HALO + i):
+            parts = [bm[r, k] for k in range(4)]
+            first(r, jnp.where(c32 < 16, pack_west(parts), pack_east(parts)))
+
+    def sweep_main(r, k, x, x0, x2, strip):
         u = x[k + 1] if k < 3 else up(x[0])
         d = x[k - 1] if k else down(x[3])
         a = [coef[f, r, k] for f in range(7)]
         return (0.2 * x[k] + a[6] + a[0] * main_east(x[k], k, strip) + a[1] * main_west(x[k], k, strip)
                 + a[2] * x2[k] + a[3] * x0[k] + a[4] * u + a[5] * d)
 
-    def sweep(j, carry):
-        p, half = lax.rem(j + 1, 2), lax.div(j, 2)
-        q = 1 - p
-
-        def block(i, carry):
-            r0 = 1 + 2 * half + 4 * i
-            rows = [[v[p, r0 + o - 1, k] for k in range(5)] for o in range(6)]
-            for o in range(4):
-                x0, x, x2 = rows[o], rows[o + 1], rows[o + 2]
-                r = r0 + o
-                new = []
-                for k in range(4):
-                    new.append(sweep_main(p, r, k, x, x0, x2, x[4]))
-                s = x[4]
-                a = [coef[f, r, 4] for f in range(7)]
-                new.append(0.2 * s + a[6] + a[0] * east(s) + a[1] * west(s) + a[2] * x2[4] + a[3] * x0[4]
-                           + a[4] * strip_up(s) + a[5] * strip_down(s))
-                for k in range(5):
-                    v[q, r, k] = new[k]
-            return carry
-
-        lax.fori_loop(0, 8 - half, block, 0)
-        return carry
-
-    lax.fori_loop(1, 8, sweep, 0)
+    def row_in(r):
+        return [v[r, k] for k in range(5)]
+
+    def sweep_row(r, x0, x, x2):
+        s = x[4]
+        for k in range(4):
+            v[r, k] = sweep_main(r, k, x, x0, x2, s)
+        a = [coef[f, r, 4] for f in range(7)]
+        v[r, 4] = (0.2 * s + a[6] + a[0] * east(s) + a[1] * west(s) + a[2] * x2[4] + a[3] * x0[4]
+                   + a[4] * strip_up(s) + a[5] * strip_down(s))
+
+    def sweep_rows(r0, n, x0, x):
+        for o in range(n):
+            x2 = row_in(r0 + o + 1)
+            sweep_row(r0 + o, x0, x, x2)
+            x0, x = x, x2
+        return x0, x
+
+    for j in range(1, 8):
+        sweep_rows(j + 1, ROWS - 2 - 2 * j, row_in(j), row_in(j + 1))
 
     def mid_join(buf, slot, row):
         block, i = row // 8, row % 8
@@ -338,15 +364,14 @@
     arrive(cond_mid)
     lo, hi = jnp.where(gx == 0, MX, 0), jnp.where(gx == ngx - 1, MX + 64, 128)
     keep_mid = (lane >= lo) & (lane < hi)
-    live = [jnp.where(gy == 0, 0.0, 1.0), 1.0, jnp.where(gy == ngy - 1, 0.0, 1.0)]
-    for row in range(MID):
+
+    def join_cond(row):
         joined = mid_join(cmx, 0, row)
         for k in range(2):
             c = jnp.where(keep_mid, joined[k], 0.0)
-            cmid[row, k] = c if row // 8 == 1 else c * live[row // 8]
-
-    def mid_coefs(i, carry):
-        r = 1 + i
+            cmid[row, k] = c if row // 8 == 1 else c * lives[row // 16]
+
+    def mid_coefs(r):
         x = [[cmid[r + d, k] for k in range(2)] for d in (-1, 0, 1)]
         u = [2.0 * harm(x[1][0], x[1][1]), 2.0 * harm(x[1][1], jnp.where(top, 0.0, up(x[1][0])))]
         for k in range(2):
@@ -359,9 +384,11 @@
                 mcoef[f, r, k] = w * faces[f]
             mcoef[6, r, k] = w
             mcoef[7, r, k] = 1.25 * diag
-        return carry
-
-    lax.fori_loop(0, MID - 2, mid_coefs, 0, unroll=2)
+
+    for row in range(7, 17):
+        join_cond(row)
+    for row in range(8, 16):
+        mid_coefs(row)
 
     for i in range(4):
         acc = cmid[8 + 2 * i, 0] + cmid[8 + 2 * i, 1] + cmid[9 + 2 * i, 0] + cmid[9 + 2 * i, 1]
@@ -379,29 +406,34 @@
     def fine_residual(i, carry):
         acc = [None, None]
         r0 = HALO + 2 * i
-        rows = [[v[1, r0 + o - 1, k] for k in range(4)] for o in range(4)]
+        rows = [[v[r0 + o - 1, k] for k in range(4)] for o in range(4)]
         for o in range(2):
             r = r0 + o
             x0, x, x2 = rows[o], rows[o + 1], rows[o + 2]
-            strip = v[1, r, 4]
+            strip = v[r, 4]
             for k in range(4):
-                res = (sweep_main(1, r, k, x, x0, x2, strip) - x[k]) * inv[r, k]
+                res = (sweep_main(r, k, x, x0, x2, strip) - x[k]) * inv[r, k]
                 acc[k // 2] = res if acc[k // 2] is None else acc[k // 2] + res
         for k in range(2):
             mvx[8 + i, k] = mcoef[6, 8 + i, k] * compact(acc[k], pair_mid)
         return carry
 
-    lax.fori_loop(0, 8, fine_residual, 0)
+    lax.fori_loop(0, 8, fine_residual, 0, unroll=4)
     mid_pack(mvx, 8, 1)
     right_mid = mid_exchange(mvx, 1)
     start(right_mid)
 
+    for row in list(range(7)) + list(range(17, MID)):
+        join_cond(row)
+    for row in list(range(1, 8)) + list(range(16, MID - 1)):
+        mid_coefs(row)
+
     def write_fine(y, carry):
         for k in range(4):
-            out_fine[pl.ds(k * 16 + y, 8, stride=64), :] = v[1, HALO + y, k]
+            out_fine[pl.ds(k * 16 + y, 8, stride=64), :] = v[HALO + y, k]
         return carry
 
-    lax.fori_loop(0, 16, write_fine, 0, unroll=4)
+    lax.fori_loop(0, 16, write_fine, 0, unroll=True)
 
     arrive(cond_low)
     for row in list(range(1, 8)) + list(range(12, 19)):
@@ -492,18 +524,21 @@
             jax.ShapeDtypeStruct((16, 8, 64), F32),
             jax.ShapeDtypeStruct((8, 4, 32), F32),
         ),
-        in_specs=[vmem] * 3,
+        in_specs=[pl.BlockSpec(memory_space=pl.ANY)] * 3,
         out_specs=(vmem,) * 3,
         scratch_shapes=[
             vec(ROWS, 4), vec(ROWS, 4),
+            vec(16), vec(16), vec(16),
             vec(16), vec(16), vec(ROWS), vec(ROWS),
             vec(ROWS), vec(ROWS), vec(ROWS),
-            vec(7, ROWS, 5), vec(ROWS, 5), vec(2, ROWS, 5),
+            vec(7, ROWS, 5), vec(ROWS, 5), vec(ROWS, 5),
             vec(MID, 2), vec(MID, 2), vec(2, 2, 4), vec(2, 3, 4), vec(2, 3, 4),
             vec(8, MID, 2), vec(MID, 2), vec(2, MID, 2),
             vec(LOW), vec(7, LOW), vec(LOW), vec(2, LOW),
             pltpu.VMEM((128, 128), F32), pltpu.VMEM((64, 128), F32),
+            pltpu.VMEM((512, 128), F32), pltpu.VMEM((512, 128), F32), pltpu.VMEM((512, 128), jnp.int32),
             pltpu.SemaphoreType.DMA((N_COPIES,)), pltpu.SemaphoreType.DMA((N_COPIES,)),
+            pltpu.SemaphoreType.DMA((3,)),
         ],
         compiler_params=pltpu.CompilerParams(
             collective_id=0, has_side_effects=True, vmem_limit_bytes=40 * 2**20),

time: 56.3 us -> 44.5 us (0.79)
  Pallas kernels: 50.6 us -> 38.9 us
    pallas_call x1, Pallas kernels: 50.6 us -> 38.9 us  [per_device(): pl.pallas_call(functools.partial(kernel, ngx, ngy), out_shape=(jax.ShapeD...]
where the time goes in v2:
time: 44.5 us; the launch traced here: 44.3 us
  Pallas kernels  38.9 us (87%)
  local copies, waits for them, and re-layouts  4.78 us (11%)
  between operations  0.65 us (1%)
    pallas_call x1, Pallas kernels, per_device(): pl.pallas_call(functools.partial(kernel, ngx, ngy), out_shape=(jax.ShapeD...  38.9 us
    unnamed x9, local copies, waits for them, and re-layouts  4.78 us

profile of v2, /device:TPU:1, one launch (start us, length us, event | category | flops | bytes accessed | tf_op | source)
XLA Modules:
  0.0 44.3 jit_solution(11061596473264944941)
XLA Ops:
  0.6 0.0 copy-start
  0.6 0.9 %copy-done = f32[32,16,128]{2,1,0:T(8,128)S(1)} copy-done((f32[32,16,128]{2,1,0:T(8,128)S(1)}, f32[32,16,128]{2,1,0:T(8,128)}, u32[]{:S(2)}) %copy-start) | copy-done | bytes 262168
  1.6 0.0 copy-start.1
  1.6 0.9 %copy-done.1 = f32[32,16,128]{2,1,0:T(8,128)S(1)} copy-done((f32[32,16,128]{2,1,0:T(8,128)S(1)}, f32[32,16,128]{2,1,0:T(8,128)}, u32[]{:S(2)}) %copy-start.1) | copy-done | bytes 262168
  2.5 0.0 copy-start.2
  2.5 0.9 %copy-done.2 = s32[32,16,128]{2,1,0:T(8,128)S(1)} copy-done((s32[32,16,128]{2,1,0:T(8,128)S(1)}, s32[32,16,128]{2,1,0:T(8,128)}, u32[]{:S(2)}) %copy-start.2) | copy-done | bytes 262168
  3.5 38.9 %shard_map.58 = (f32[512,128]{1,0:T(8,128)S(1)}, f32[16,8,64]{2,1,0:T(8,128)S(1)}, f32[8,4,32]{2,1,0:T(4,128)S(1)}) custom-call(f32[512,128]{1,0:T(8,128)S(1)} %bitcast.4, f32[512,128]{1,0:T(8,128)S(1)} %bitcast.5, s32[512,128]{1,0:T(8,128)S(1)} %bitcast.6), custom_call_target="tpu_custom_call" | custom-call | tf_op jit(solution)/shard_map/pallas_call | solution.py:520
  42.4 0.7 %copy.9 = f32[32,16,128]{2,1,0:T(8,128)} copy(f32[32,16,128]{2,1,0:T(8,128)S(1)} %bitcast.7) | data formatting | bytes 524288
  43.1 0.6 %copy.10 = f32[16,8,64]{2,1,0:T(8,128)} copy(f32[16,8,64]{2,1,0:T(8,128)S(1)} %get-tuple-element.13) | data formatting | bytes 65536
  43.7 0.6 %copy.11 = f32[8,4,32]{2,1,0:T(4,128)} copy(f32[8,4,32]{2,1,0:T(4,128)S(1)} %get-tuple-element.14) | data formatting | bytes 8192
Async XLA Ops:
  0.6 1.0 %copy-start = (f32[32,16,128]{2,1,0:T(8,128)S(1)}, f32[32,16,128]{2,1,0:T(8,128)}, u32[]{:S(2)}) copy-start(f32[32,16,128]{2,1,0:T(8,128)} %param.3) | copy-start | bytes 786436
  1.6 0.9 %copy-start.1 = (f32[32,16,128]{2,1,0:T(8,128)S(1)}, f32[32,16,128]{2,1,0:T(8,128)}, u32[]{:S(2)}) copy-start(f32[32,16,128]{2,1,0:T(8,128)} %param.4) | copy-start | bytes 786436
  2.5 0.9 %copy-start.2 = (s32[32,16,128]{2,1,0:T(8,128)S(1)}, s32[32,16,128]{2,1,0:T(8,128)}, u32[]{:S(2)}) copy-start(s32[32,16,128]{2,1,0:T(8,128)} %param.5) | copy-start | bytes 786436

commit v3 on v2

--- a/solution.py
+++ b/solution.py
@@ -145,26 +145,31 @@
         l.wait()
 
     def load_pair(i, carry):
-        acc = [None, None]
         for o in range(2):
             y = 2 * i + o
             conds, rights = [], []
             for k in range(4):
-                p, m = take(perm, y, k), take(mask, y, k)
-                c = jnp.where(m == 2, 0.0, p)
+                m = take(mask, y, k)
+                c = jnp.where(m == 2, 0.0, take(perm, y, k))
                 b = jnp.where(m == 1, take(source, y, k), 0.0)
                 cm[HALO + y, k] = c
                 bm[HALO + y, k] = b
                 conds.append(c)
                 rights.append(b)
-                term = LEAK * p + (1.0 - LEAK) * c
-                acc[k // 2] = term if acc[k // 2] is None else acc[k // 2] + term
             aw, ae = pack_west(conds), pack_east(conds)
             bw, be = pack_west(rights), pack_east(rights)
             own_w[y], own_e[y] = aw, ae
             own_b[y] = jnp.where(c32 < 16, bw, be)
             sr[y] = jnp.where(c32 < 16, aw, roll(bw, 16))
             sl[y] = jnp.where(c32 >= 16, ae, roll(be, 112))
+        return carry
+
+    def cond_pair(i, carry):
+        acc = [None, None]
+        for y in (2 * i, 2 * i + 1):
+            for k in range(4):
+                term = LEAK * take(perm, y, k) + (1.0 - LEAK) * cm[HALO + y, k]
+                acc[k // 2] = term if acc[k // 2] is None else acc[k // 2] + term
         for k in range(2):
             cmx[8 + i, k] = compact(acc[k], pair_mid) * 0.125
         return carry
@@ -177,7 +182,6 @@
             midx[slot, 0, i] = groups(parts, [32 * q - (MX + 42) for q in range(4)])
             midx[slot, 1, i] = groups(parts, [32 * q - MX for q in range(4)])
 
-    mid_pack(cmx, 8, 0)
     pl.semaphore_wait(barrier, len(around))
 
     def start(cs_):
@@ -197,25 +201,26 @@
             got.append(copy(src.at[pl.ds(0, n)], dst.at[pl.ds(n + own, n)], (dx, -1)))
         return got
 
-    def edges(buf, n, own, first=0):
-        return [copy(buf.at[pl.ds(first + own, n)], buf.at[pl.ds(first, n)], (0, 1)),
-                copy(buf.at[pl.ds(first + n, n)], buf.at[pl.ds(first + n + own, n)], (0, -1))]
-
-    cond_y = edges(cm, HALO, 16)
+    def edges(buf, n, own, halo):
+        return [copy(buf.at[pl.ds(halo + own - n, n)], buf.at[pl.ds(halo - n, n)], (0, 1)),
+                copy(buf.at[pl.ds(halo, n)], buf.at[pl.ds(halo + own, n)], (0, -1))]
+
+    cond_y = edges(cm, HALO, 16, HALO)
     raw_x = strips(sr, sl, rl, rr, HALO)
-    right_y = edges(bm, HALO, 16)
-    start(cond_y + raw_x + right_y)
+    right_y = edges(bm, HALO - 1, 16, HALO)
+    start(cond_y + raw_x)
 
     def mid_exchange(buf, slot):
-        got = edges(buf, 8, 8)
-        for dx, side, dst in ((1, 0, mrl), (-1, 1, mrr)):
-            src = midx.at[slot, side]
-            for dy, block in ((0, 1), (1, 0), (-1, 2)):
-                got.append(copy(src, dst.at[slot, block], (dx, dy)))
-        return got
-
+        got = []
+        for block, dy in ((0, 1), (2, -1), (1, 0)):
+            for dx, side, dst in ((1, 0, mrl), (-1, 1, mrr)):
+                got.append(copy(midx.at[slot, side], dst.at[slot, block], (dx, dy)))
+        return got[:4] + edges(buf, 8, 8, 8) + got[4:]
+
+    lax.fori_loop(0, 8, cond_pair, 0, unroll=4)
+    mid_pack(cmx, 8, 0)
     cond_mid = mid_exchange(cmx, 0)
-    start(cond_mid)
+    start(cond_mid + right_y)
 
     inside = jnp.where(gx == 0, 9, 0), jnp.where(gx == ngx - 1, 23, 32)
     keep = (c32 >= inside[0]) & (c32 < inside[1])
@@ -313,44 +318,6 @@
         for r in (1 + i, 15 + HALO + i):
             fine_coefs(r)
 
-    arrive(right_y)
-    first(HALO, own_b[0])
-    first(HALO + 15, own_b[15])
-
-    @loop(HALO - 1, 4)
-    def _(i):
-        for r in (1 + i, 16 + HALO + i):
-            parts = [bm[r, k] for k in range(4)]
-            first(r, jnp.where(c32 < 16, pack_west(parts), pack_east(parts)))
-
-    def sweep_main(r, k, x, x0, x2, strip):
-        u = x[k + 1] if k < 3 else up(x[0])
-        d = x[k - 1] if k else down(x[3])
-        a = [coef[f, r, k] for f in range(7)]
-        return (0.2 * x[k] + a[6] + a[0] * main_east(x[k], k, strip) + a[1] * main_west(x[k], k, strip)
-                + a[2] * x2[k] + a[3] * x0[k] + a[4] * u + a[5] * d)
-
-    def row_in(r):
-        return [v[r, k] for k in range(5)]
-
-    def sweep_row(r, x0, x, x2):
-        s = x[4]
-        for k in range(4):
-            v[r, k] = sweep_main(r, k, x, x0, x2, s)
-        a = [coef[f, r, 4] for f in range(7)]
-        v[r, 4] = (0.2 * s + a[6] + a[0] * east(s) + a[1] * west(s) + a[2] * x2[4] + a[3] * x0[4]
-                   + a[4] * strip_up(s) + a[5] * strip_down(s))
-
-    def sweep_rows(r0, n, x0, x):
-        for o in range(n):
-            x2 = row_in(r0 + o + 1)
-            sweep_row(r0 + o, x0, x, x2)
-            x0, x = x, x2
-        return x0, x
-
-    for j in range(1, 8):
-        sweep_rows(j + 1, ROWS - 2 - 2 * j, row_in(j), row_in(j + 1))
-
     def mid_join(buf, slot, row):
         block, i = row // 8, row % 8
         out = []
@@ -402,6 +369,44 @@
 
     cond_low = low_exchange(clow)
     start(cond_low)
+
+    arrive(right_y)
+    first(HALO, own_b[0])
+    first(HALO + 15, own_b[15])
+
+    @loop(HALO - 1, 4)
+    def _(i):
+        for r in (1 + i, 16 + HALO + i):
+            parts = [bm[r, k] for k in range(4)]
+            first(r, jnp.where(c32 < 16, pack_west(parts), pack_east(parts)))
+
+    def sweep_main(r, k, x, x0, x2, strip):
+        u = x[k + 1] if k < 3 else up(x[0])
+        d = x[k - 1] if k else down(x[3])
+        a = [coef[f, r, k] for f in range(7)]
+        return (0.2 * x[k] + a[6] + a[0] * main_east(x[k], k, strip) + a[1] * main_west(x[k], k, strip)
+                + a[2] * x2[k] + a[3] * x0[k] + a[4] * u + a[5] * d)
+
+    def row_in(r):
+        return [v[r, k] for k in range(5)]
+
+    def sweep_row(r, x0, x, x2):
+        s = x[4]
+        for k in range(4):
+            v[r, k] = sweep_main(r, k, x, x0, x2, s)
+        a = [coef[f, r, 4] for f in range(7)]
+        v[r, 4] = (0.2 * s + a[6] + a[0] * east(s) + a[1] * west(s) + a[2] * x2[4] + a[3] * x0[4]
+                   + a[4] * strip_up(s) + a[5] * strip_down(s))
+
+    def sweep_rows(r0, n, x0, x):
+        for o in range(n):
+            x2 = row_in(r0 + o + 1)
+            sweep_row(r0 + o, x0, x, x2)
+            x0, x = x, x2
+        return x0, x
+
+    for j in range(1, 8):
+        sweep_rows(j + 1, ROWS - 2 - 2 * j, row_in(j), row_in(j + 1))
 
     def fine_residual(i, carry):
         acc = [None, None]
@@ -511,6 +516,18 @@
 
 
 N_COPIES = 2 + 6 + 2 + 8 + 4 + 8 + 4
+
+
+def hand_on(a, b, c, out_a, out_b, out_c, held_a, held_b, held_c, sem):
+    ways = ((a, held_a, out_a), (b, held_b, out_b), (c, held_c, out_c))
+    copies = [[pltpu.make_async_copy(x, y, sem.at[0, i]), pltpu.make_async_copy(y, z, sem.at[1, i])] for i, (x, y, z) in enumerate(ways)]
+    for first, _ in copies:
+        first.start()
+    for first, second in copies:
+        first.wait()
+        second.start()
+    for _, second in copies:
+        second.wait()
 
 
 def per_device(ngx, ngy, permeability, source, phase_mask):
@@ -541,8 +558,18 @@
             pltpu.SemaphoreType.DMA((3,)),
         ],
         compiler_params=pltpu.CompilerParams(
-            collective_id=0, has_side_effects=True, vmem_limit_bytes=40 * 2**20),
+            collective_id=0, has_side_effects=True, vmem_limit_bytes=62 * 2**20),
     )(*flat)
+    whole = pl.BlockSpec(memory_space=pl.ANY)
+    results = (fine, mid, low)
+    fine, mid, low = pl.pallas_call(
+        hand_on,
+        out_shape=tuple(jax.ShapeDtypeStruct(x.shape, F32) for x in results),
+        in_specs=[whole] * 3,
+        out_specs=(whole,) * 3,
+        scratch_shapes=[pltpu.VMEM(x.shape, F32) for x in results] + [pltpu.SemaphoreType.DMA((2, 3))],
+        compiler_params=pltpu.CompilerParams(vmem_limit_bytes=62 * 2**20),
+    )(*results)
     return fine.reshape(32, 16, 128), mid, low
 
 

time: 44.5 us -> 42.1 us (0.946)
  local copies, waits for them, and re-layouts: 4.78 us -> 0 us
  Pallas kernels: 38.9 us -> 41.3 us
    unnamed x9 -> x0, local copies, waits for them, and re-layouts: 4.78 us -> none
    pallas_call x0 -> x1, Pallas kernels: none -> 1.72 us  [per_device(): pl.pallas_call(hand_on, out_shape=tuple((jax.ShapeDtypeStruct(x.shape, F3...]
    pallas_call x1, Pallas kernels: 38.9 us -> 39.6 us  [per_device(): pl.pallas_call(functools.partial(kernel, ngx, ngy), out_shape=(jax.ShapeD...]
where the time goes in v3:
time: 42.1 us; the launch traced here: 41.9 us
  Pallas kernels  41.3 us (98%)
  between operations  0.64 us (2%)
    pallas_call x1, Pallas kernels, per_device(): pl.pallas_call(functools.partial(kernel, ngx, ngy), out_shape=(jax.ShapeD...  39.6 us
    pallas_call x1, Pallas kernels, per_device(): pl.pallas_call(hand_on, out_shape=tuple((jax.ShapeDtypeStruct(x.shape, F3...  1.72 us

profile of v3, /device:TPU:1, one launch (start us, length us, event | category | flops | bytes accessed | tf_op | source)
XLA Modules:
  0.0 41.9 jit_solution(16183695123104229391)
XLA Ops:
  0.6 39.6 %shard_map.58 = (f32[512,128]{1,0:T(8,128)}, f32[16,8,64]{2,1,0:T(8,128)}, f32[8,4,32]{2,1,0:T(4,128)}) custom-call(f32[512,128]{1,0:T(8,128)} %bitcast.4, f32[512,128]{1,0:T(8,128)} %bitcast.5, s32[512,128]{1,0:T(8,128)} %bitcast.6), custom_call_target="tpu_custom_call" | custom-call | tf_op jit(solution)/shard_map/pallas_call | solution.py:537
  40.2 1.7 %shard_map.59 = (f32[512,128]{1,0:T(8,128)}, f32[16,8,64]{2,1,0:T(8,128)}, f32[8,4,32]{2,1,0:T(4,128)}) custom-call(f32[512,128]{1,0:T(8,128)} %get-tuple-element.9.a, f32[16,8,64]{2,1,0:T(8,128)} %get-tuple-element.10.b, f32[8,4,32]{2,1,0:T(4,128)} %get-tuple-element.11.c), custom_call_target="tpu_custom_call" | custom-call | tf_op jit(solution)/shard_map/pallas_call | solution.py:565

commit v4 on v3

--- a/solution.py
+++ b/solution.py
@@ -104,7 +104,7 @@
 
 def kernel(ngx, ngy, perm_in, source_in, mask_in, out_fine, out_mid, out_low,
            cm, bm, own_w, own_e, own_b, sr, sl, rl, rr, cs, cse, csw, coef, inv, v,
-           cmx, cmid, midx, mrl, mrr, mcoef, mvx, mv, clow, lcoef, lvx, lv, tmid, tlow, perm, source, mask, send, recv, load):
+           cmx, cmid, midx, mrl, mrr, mcoef, mvx, mv, clow, lcoef, lvx, lv, tfine, tmid, tmid64, tlow, perm, source, mask, send, recv, load, store):
     gx, gy = lax.axis_index("gx"), lax.axis_index("gy")
     loads = [pltpu.make_async_copy(a, b, load.at[i])
              for i, (a, b) in enumerate(((perm_in, perm), (mask_in, mask), (source_in, source)))]
@@ -291,7 +291,7 @@
     def _(i):
         fine_coefs(HALO + 1 + i)
 
-    @loop(14, 7)
+    @loop(14, True)
     def _(i):
         first(HALO + 1 + i, own_b[1 + i])
 
@@ -374,7 +374,7 @@
     first(HALO, own_b[0])
     first(HALO + 15, own_b[15])
 
-    @loop(HALO - 1, 4)
+    @loop(HALO - 1, True)
     def _(i):
         for r in (1 + i, 16 + HALO + i):
             parts = [bm[r, k] for k in range(4)]
@@ -435,10 +435,12 @@
 
     def write_fine(y, carry):
         for k in range(4):
-            out_fine[pl.ds(k * 16 + y, 8, stride=64), :] = v[HALO + y, k]
+            tfine[pl.ds(k * 16 + y, 8, stride=64), :] = v[HALO + y, k]
         return carry
 
     lax.fori_loop(0, 16, write_fine, 0, unroll=True)
+    stores = [pltpu.make_async_copy(tfine, out_fine, store.at[0]), pltpu.make_async_copy(tmid64, out_mid, store.at[1])]
+    stores[0].start()
 
     arrive(cond_low)
     for row in list(range(1, 8)) + list(range(12, 19)):
@@ -497,7 +499,8 @@
     for i in range(8):
         for k in range(2):
             tmid[pl.ds(k * 8 + i, 8, stride=16), :] = roll(mv[1, 8 + i, k], -MX)
-    out_mid[...] = tmid[...].reshape(16, 8, 128)[:, :, :64]
+    tmid64[...] = tmid[...].reshape(16, 8, 128)[:, :, :64]
+    stores[1].start()
 
     arrive(right_low)
     for j in range(1, 8):
@@ -511,6 +514,8 @@
         tlow[pl.ds(i, 8, stride=8), :] = roll(lv[1, 8 + i], -LX)
     out_low[...] = tlow[...].reshape(8, 8, 128)[:, :4, :32]
 
+    for c_ in stores:
+        c_.wait()
     for c_ in cond_y + raw_x + right_y + cond_mid + cond_low + right_mid + right_low:
         c_.wait_send()
 
@@ -518,9 +523,15 @@
 N_COPIES = 2 + 6 + 2 + 8 + 4 + 8 + 4
 
 
+PIECES = 4
+
+
 def hand_on(a, b, c, out_a, out_b, out_c, held_a, held_b, held_c, sem):
-    ways = ((a, held_a, out_a), (b, held_b, out_b), (c, held_c, out_c))
-    copies = [[pltpu.make_async_copy(x, y, sem.at[0, i]), pltpu.make_async_copy(y, z, sem.at[1, i])] for i, (x, y, z) in enumerate(ways)]
+    n = a.shape[0] // PIECES
+    ways = [tuple(x.at[pl.ds(n * i, n)] for x in (a, held_a, out_a)) for i in range(PIECES)]
+    ways += [(b, held_b, out_b), (c, held_c, out_c)]
+    copies = [(pltpu.make_async_copy(x, y, sem.at[0, i]), pltpu.make_async_copy(y, z, sem.at[1, i]))
+              for i, (x, y, z) in enumerate(ways)]
     for first, _ in copies:
         first.start()
     for first, second in copies:
@@ -542,7 +553,7 @@
             jax.ShapeDtypeStruct((8, 4, 32), F32),
         ),
         in_specs=[pl.BlockSpec(memory_space=pl.ANY)] * 3,
-        out_specs=(vmem,) * 3,
+        out_specs=(pl.BlockSpec(memory_space=pl.ANY),) * 2 + (vmem,),
         scratch_shapes=[
             vec(ROWS, 4), vec(ROWS, 4),
             vec(16), vec(16), vec(16),
@@ -552,10 +563,11 @@
             vec(MID, 2), vec(MID, 2), vec(2, 2, 4), vec(2, 3, 4), vec(2, 3, 4),
             vec(8, MID, 2), vec(MID, 2), vec(2, MID, 2),
             vec(LOW), vec(7, LOW), vec(LOW), vec(2, LOW),
-            pltpu.VMEM((128, 128), F32), pltpu.VMEM((64, 128), F32),
+            pltpu.VMEM((512, 128), F32), pltpu.VMEM((128, 128), F32),
+            pltpu.VMEM((16, 8, 64), F32), pltpu.VMEM((64, 128), F32),
             pltpu.VMEM((512, 128), F32), pltpu.VMEM((512, 128), F32), pltpu.VMEM((512, 128), jnp.int32),
             pltpu.SemaphoreType.DMA((N_COPIES,)), pltpu.SemaphoreType.DMA((N_COPIES,)),
-            pltpu.SemaphoreType.DMA((3,)),
+            pltpu.SemaphoreType.DMA((3,)), pltpu.SemaphoreType.DMA((2,)),
         ],
         compiler_params=pltpu.CompilerParams(
             collective_id=0, has_side_effects=True, vmem_limit_bytes=62 * 2**20),
@@ -567,7 +579,7 @@
         out_shape=tuple(jax.ShapeDtypeStruct(x.shape, F32) for x in results),
         in_specs=[whole] * 3,
         out_specs=(whole,) * 3,
-        scratch_shapes=[pltpu.VMEM(x.shape, F32) for x in results] + [pltpu.SemaphoreType.DMA((2, 3))],
+        scratch_shapes=[pltpu.VMEM(x.shape, F32) for x in results] + [pltpu.SemaphoreType.DMA((2, PIECES + 2))],
         compiler_params=pltpu.CompilerParams(vmem_limit_bytes=62 * 2**20),
     )(*results)
     return fine.reshape(32, 16, 128), mid, low

time: 42.1 us -> 41.8 us (level)
  no operation moved by 1% of the time
where the time goes in v4:
time: 41.8 us; the launch traced here: 41.6 us
  Pallas kernels  41 us (98%)
  between operations  0.64 us (2%)
    pallas_call x1, Pallas kernels, per_device(): pl.pallas_call(functools.partial(kernel, ngx, ngy), out_shape=(jax.ShapeD...  39.3 us
    pallas_call x1, Pallas kernels, per_device(): pl.pallas_call(hand_on, out_shape=tuple((jax.ShapeDtypeStruct(x.shape, F3...  1.7 us

profile of v4, /device:TPU:1, one launch (start us, length us, event | category | flops | bytes accessed | tf_op | source)
XLA Modules:
  0.0 41.6 jit_solution(4149786576361336434)
XLA Ops:
  0.6 39.3 %shard_map.58 = (f32[512,128]{1,0:T(8,128)}, f32[16,8,64]{2,1,0:T(8,128)}, f32[8,4,32]{2,1,0:T(4,128)}) custom-call(f32[512,128]{1,0:T(8,128)} %bitcast.4, f32[512,128]{1,0:T(8,128)} %bitcast.5, s32[512,128]{1,0:T(8,128)} %bitcast.6), custom_call_target="tpu_custom_call" | custom-call | tf_op jit(solution)/shard_map/pallas_call | solution.py:548
  39.9 1.7 %shard_map.59 = (f32[512,128]{1,0:T(8,128)}, f32[16,8,64]{2,1,0:T(8,128)}, f32[8,4,32]{2,1,0:T(4,128)}) custom-call(f32[512,128]{1,0:T(8,128)} %get-tuple-element.9.a, f32[16,8,64]{2,1,0:T(8,128)} %get-tuple-element.10.b, f32[8,4,32]{2,1,0:T(4,128)} %get-tuple-element.11.c), custom_call_target="tpu_custom_call" | custom-call | tf_op jit(solution)/shard_map/pallas_call | solution.py:577
